TPU v7x, 128 devices: a whole 4x4x4 slice. The times are simulated.
128 devices in a mesh: seq: 16 (over z, x_lo, core), tp: 8 (over x_hi, y).
Axes of the slice: x: 4 (x_hi: 2, x_lo: 2; x = x_hi * 2 + x_lo), y: 4, z: 4, core: 2. Of those that a mesh axis runs over, the one named last changes fastest.
Arguments:
- tokens: bfloat16 [8192, 4096], P(('seq', 'tp')), may hold values from -6 to 6
- norm_gain: float32 [4096], replicated, may hold values from 0.1 to 1.9
- in_weight: bfloat16 [4096, 3, 4096], P('seq', None, 'tp'), may hold values from -0.09375 to 0.09375
- short_filter: float32 [7, 3, 4096], P(None, None, 'tp'), may hold values from -2.4 to 2.4
- long_filter: float32 [128, 4096], P(None, 'tp'), may hold values from -0.6 to 0.6
- skip_gain: float32 [4096], P('tp'), may hold values from -4 to 4
- out_weight: bfloat16 [4096, 4096], P('tp', 'seq'), may hold values from -0.09375 to 0.09375
Outputs:
- mixed: bfloat16 [8192, 4096], P(('seq', 'tp'))
All inputs are finite; a program needn't handle non-finite values.
Results may differ from a plain program's by a relative error of at most 0.02.
Values may be sent and summed in bfloat16 or wider, within the bound.
A program may use at most 256 MiB of HBM per device.

v0:
```python
import jax
import jax.numpy as jnp
from jax import lax
from jax.sharding import PartitionSpec as P


def passed_along(x, axis, by):
    count = lax.axis_size(axis)
    pairs = [(i, i + by) for i in range(count) if 0 <= i + by < count]
    return lax.ppermute(x, axis, pairs)


def featurize(extended, short_filter):
    taps = short_filter.shape[0]
    out_rows = extended.shape[0] - (taps - 1)
    widened = extended.astype(jnp.float32)
    total = jnp.zeros((out_rows,) + extended.shape[1:], jnp.float32)
    for delay in range(taps):
        total = (
            total + short_filter[delay] * widened[taps - 1 - delay : taps - 1 - delay + out_rows]
        )
    return total


def on_device(tokens, norm_gain, in_weight, short_filter, long_filter, skip_gain, out_weight):
    widened = tokens.astype(jnp.float32)
    mean_square = jnp.mean(widened * widened, axis=-1, keepdims=True)
    normed = (widened * lax.rsqrt(mean_square + 1e-06) * norm_gain).astype(jnp.bfloat16)
    in_whole = lax.all_gather(in_weight, "seq", axis=0, tiled=True)
    channels = in_whole.shape[2]
    in_matrix = in_whole.reshape(in_whole.shape[0], 3 * channels)
    branches = jnp.dot(
        lax.all_gather(normed, "tp", axis=0, tiled=True),
        in_matrix,
        preferred_element_type=jnp.float32,
    ).astype(jnp.bfloat16)
    block = branches.shape[0]
    branches = branches.reshape(block, 3, channels)
    taps_long = long_filter.shape[0]
    taps_short = short_filter.shape[0]
    before = passed_along(branches[block - (taps_short - 1) :], "seq", 1)
    featured = featurize(jnp.concatenate([before, branches], axis=0), short_filter)
    gated = (featured[:, 1] * featured[:, 2]).astype(jnp.bfloat16)
    gated_before = passed_along(gated[block - (taps_long - 1) :], "seq", 1)
    gated_ext = jnp.concatenate([gated_before, gated], axis=0)
    query_part = featured[:, 0]
    gated_wide = gated_ext.astype(jnp.float32)
    filtered = skip_gain * gated_wide[taps_long - 1 :]
    for first_tap in range(0, taps_long, 16):
        stacked = jnp.stack(
            [
                gated_wide[taps_long - 1 - lagged : taps_long - 1 - lagged + block]
                for lagged in range(first_tap, first_tap + 16)
            ]
        )
        filtered = filtered + jnp.einsum(
            "jtc,jc->tc", stacked, long_filter[first_tap : first_tap + 16]
        )
    mixed_in = (query_part * filtered).astype(jnp.bfloat16)
    out_whole = lax.all_gather(out_weight, "seq", axis=1, tiled=True)
    summed = lax.psum_scatter(
        jnp.dot(mixed_in, out_whole, preferred_element_type=jnp.float32).astype(jnp.bfloat16),
        "tp",
        scatter_dimension=0,
        tiled=True,
    ).astype(jnp.float32)
    return (widened + summed).astype(jnp.bfloat16)


def solution(mesh):
    placed = (
        P(("seq", "tp"), None),
        P(),
        P("seq", None, "tp"),
        P(None, None, "tp"),
        P(None, "tp"),
        P("tp"),
        P("tp", "seq"),
    )
    return jax.shard_map(
        on_device, mesh=mesh, in_specs=placed, out_specs=P(("seq", "tp"), None), check_vma=False
    )
```

profile of v0, /device:TPU:0, one launch (start us, length us, event | category | flops | bytes accessed | tf_op | source)
XLA Modules:
  0.0 439.5 jit_solution(18142066823974303935)
XLA Ops:
  6.5 1.2 fusion.22
  7.8 2.0 fusion.24
  9.9 2.3 copy.10
  13.0 1.2 fusion.158
  14.2 0.9 slice_bitcast_fusion.136
  15.8 68.0 %all-gather.4.cloned.1.call-done = bf16[512,4096]{1,0:T(8,128)(2,1)} async-done(((bf16[64,4096]{1,0:T(8,128)(2,1)}), bf16[512,4096]{1,0:T(8,128)(2,1)}) %all-gather.4.cloned.1.call-update) | async-done | bytes 4194320 | tf_op jit(solution)/shard_map/all_gather | solution.py:33
  83.8 79.0 %all-gather.6.cloned.1.call-done = bf16[4096,3,512]{0,2,1:T(8,128)(2,1)} async-done(((bf16[256,3,512]{0,2,1:T(8,128)(2,1)}), bf16[4096,3,512]{0,2,1:T(8,128)(2,1)}) %all-gather.6.cloned.1.call-update) | async-done | bytes 12582928 | tf_op jit(solution)/shard_map/all_gather | solution.py:29
  162.8 10.9 %convolution_convert_fusion.1 = bf16[512,1536]{1,0:T(8,128)(2,1)S(1)} fusion(bf16[512,4096]{1,0:T(8,128)(2,1)} %all-gather.4.cloned.1.call-done, bf16[4096,1536]{0,1:T(8,128)(2,1)} %bitcast.624), kind=kOutput, calls=%fused_computation.30 | convolution fusion | flops 6443237376 | bytes 18350080 | tf_op jit(solution)/shard_map/dot_general | solution.py:32
  173.7 1.0 copy.39
  174.7 2.2 collective-permute-start
  178.1 0.9 copy.22
  179.0 0.9 copy.19
  180.7 0.9 copy.34
  181.6 0.9 copy.31
  183.4 0.9 copy.25
  184.3 0.9 copy.37
  186.7 7.9 %fusion.16 = f32[512,3,512]{0,2,1:T(8,128)S(1)} fusion(f32[518,3,512]{0,2,1:T(8,128)S(1)} %maximum_convert_fusion, f32[3,512]{1,0:T(4,128)S(1)} %get-tuple-element.147, f32[3,512]{1,0:T(4,128)S(1)} %get-tuple-element.148, f32[3,512]{1,0:T(4,128)} %get-tuple-element.149, f32[3,512]{1,0:T(4,128)} %get-tuple-element.150, f32[3,512]{1,0:T(4,128)} %get-tuple-element.151, ...), kind=kLoop, calls=%fused_computation.18 | loop fusion | flops 10223616 | bytes 25208832 | tf_op jit(solution)/shard_map/add | solution.py:20
  194.9 4.5 %collective-permute-start.1 = (bf16[127,512]{0,1:T(8,128)(2,1)S(1)}, bf16[127,512]{0,1:T(8,128)(2,1)S(1)}, u32[]{:S(2)}, u32[]{:S(2)}) collective-permute-start(bf16[127,512]{0,1:T(8,128)(2,1)S(1)} %slice_bitcast_fusion.128), channel_id=1, source_target_pairs={{0,8},{8,16},{16,24},{24,32},{32,40},{40,48},{48,56},{56,64},{64,7... | collective-permute-start | bytes 390152 | tf_op jit(solution)/shard_map/ppermute | solution.py:10
  200.5 2.6 fusion.137
  203.1 1.1 bitcast_dynamic-update-slice_fusion
  204.2 3.0 fusion.152
  207.2 3.1 fusion.151
  210.3 3.0 fusion.150
  213.3 3.0 fusion.149
  216.3 3.0 fusion.148
  219.2 3.0 fusion.147
  222.2 2.9 fusion.146
  225.2 3.2 fusion.145
  228.4 3.0 fusion.144
  231.4 3.0 fusion.143
  234.4 3.0 fusion.142
  237.4 3.0 fusion.141
  240.3 3.0 fusion.140
  243.3 3.3 copy-done.12
  246.6 3.2 fusion.139
  249.7 3.1 fusion.138
  252.9 3.2 copy-done.11
  256.1 8.9 %fusion.10 = f32[512,1,512]{2,1,0:T(1,128)S(1)} fusion(bf16[16,512,1]{0,2,1:T(2,128)(2,1)S(1)} %copy-done.9, bf16[16,512,512]{1,2,0:T(8,128)(2,1)} %get-tuple-element.11), kind=kOutput, calls=%fused_computation.10 | convolution fusion | flops 8388608 | bytes 9453568 | tf_op jit(solution)/shard_map/jtc,jc->tc/dot_general | solution.py:56
  265.0 9.5 %fusion.12 = f32[512,1,512]{2,1,0:T(1,128)} fusion(bf16[16,512,1]{0,2,1:T(2,128)(2,1)S(1)} %copy-done.8, bf16[16,512,512]{1,2,0:T(8,128)(2,1)} %copy-done.11), kind=kOutput, calls=%fused_computation.12 | convolution fusion | flops 8388608 | bytes 9453568 | tf_op jit(solution)/shard_map/jtc,jc->tc/dot_general | solution.py:56
  274.5 9.7 %fusion.14 = f32[512,1,512]{2,1,0:T(1,128)} fusion(bf16[16,512,1]{0,2,1:T(2,128)(2,1)S(1)} %copy-done.7, bf16[16,512,512]{1,2,0:T(8,128)(2,1)} %get-tuple-element.5), kind=kOutput, calls=%fused_computation.14 | convolution fusion | flops 8388608 | bytes 9453568 | tf_op jit(solution)/shard_map/jtc,jc->tc/dot_general | solution.py:56
  284.2 9.5 %fusion.2 = f32[512,1,512]{2,1,0:T(1,128)} fusion(bf16[16,512,1]{0,2,1:T(2,128)(2,1)S(1)} %copy-done.6, bf16[16,512,512]{1,2,0:T(8,128)(2,1)} %get-tuple-element.7), kind=kOutput, calls=%fused_computation.2 | convolution fusion | flops 8388608 | bytes 9453568 | tf_op jit(solution)/shard_map/jtc,jc->tc/dot_general | solution.py:56
  293.7 9.5 %fusion.4 = f32[512,1,512]{2,1,0:T(1,128)} fusion(bf16[16,512,1]{0,2,1:T(2,128)(2,1)S(1)} %copy-done.5, bf16[16,512,512]{1,2,0:T(8,128)(2,1)} %get-tuple-element.8), kind=kOutput, calls=%fused_computation.4 | convolution fusion | flops 8388608 | bytes 9453568 | tf_op jit(solution)/shard_map/jtc,jc->tc/dot_general | solution.py:56
  303.3 9.7 %fusion.6 = f32[512,1,512]{2,1,0:T(1,128)} fusion(bf16[16,512,1]{0,2,1:T(2,128)(2,1)S(1)} %copy-done.4, bf16[16,512,512]{1,2,0:T(8,128)(2,1)} %get-tuple-element.9), kind=kOutput, calls=%fused_computation.6 | convolution fusion | flops 8388608 | bytes 9453568 | tf_op jit(solution)/shard_map/jtc,jc->tc/dot_general | solution.py:56
  313.0 9.5 %fusion.8 = f32[512,1,512]{2,1,0:T(1,128)} fusion(bf16[16,512,1]{0,2,1:T(2,128)(2,1)S(1)} %copy-done.3, bf16[16,512,512]{1,2,0:T(8,128)(2,1)} %get-tuple-element.10), kind=kOutput, calls=%fused_computation.8 | convolution fusion | flops 8388608 | bytes 9453568 | tf_op jit(solution)/shard_map/jtc,jc->tc/dot_general | solution.py:56
  322.5 9.7 %fusion = f32[512,1,512]{2,1,0:T(1,128)} fusion(bf16[16,512,1]{0,2,1:T(2,128)(2,1)S(1)} %copy-done.2, bf16[16,512,512]{1,2,0:T(8,128)(2,1)} %get-tuple-element.6), kind=kOutput, calls=%fused_computation | convolution fusion | flops 8388608 | bytes 9453568 | tf_op jit(solution)/shard_map/jtc,jc->tc/dot_general | solution.py:56
  332.3 10.1 %convolution_convert_fusion = bf16[512,4096]{1,0:T(8,128)(2,1)} fusion(bf16[512,4096]{1,0:T(8,128)(2,1)} %all-gather.8.cloned.1.call-done, f32[512,3,512]{0,2,1:T(8,128)} %copy-done, f32[512,1,512]{2,1,0:T(1,128)} %fusion, f32[512,1,512]{2,1,0:T(1,128)} %fusion.2, f32[512,1,512]{2,1,0:T(1,128)} %fusion.4, f32[512,1,512]{2,1,0:T(1,128)} %fusion.6, ...), kind=kOutput, calls=%fused_computation.16 | convolution fusion | flops 2152464384 | bytes 18876416 | tf_op jit(solution)/shard_map/dot_general | solution.py:62
  342.4 88.1 %reduce-scatter.2.cloned.1.call-done = bf16[64,4096]{1,0:T(8,128)(2,1)} async-done(((bf16[512,4096]{1,0:T(8,128)(2,1)}), bf16[64,4096]{1,0:T(8,128)(2,1)}) %reduce-scatter.2.cloned.1.call-update) | async-done | bytes 524304 | tf_op jit(solution)/shard_map/reduce_scatter | solution.py:61
  430.5 2.0 fusion.25
  (49 shorter events, 7.4 us)
Async XLA Ops:
  6.5 77.2 %all-gather.4.cloned.1.call-start = ((), (), s32[]{:S(2)}) async-start(), calls=%async_computation.1 | async-start | bytes 4718592 | tf_op jit(solution)/shard_map/all_gather | solution.py:33
  9.9 152.9 %all-gather.6.cloned.1.call-start = ((), (), s32[]{:S(2)}) async-start(), calls=%async_computation.2 | async-start | bytes 13369344 | tf_op jit(solution)/shard_map/all_gather | solution.py:29
  12.2 320.0 %all-gather.8.cloned.1.call-start = ((), (), s32[]{:S(2)}) async-start(), calls=%async_computation.3 | async-start | bytes 4456448 | tf_op jit(solution)/shard_map/all_gather | solution.py:60
  13.0 417.6 %reduce-scatter.2.cloned.1.call-start = ((), (), s32[]{:S(2)}) async-start(), calls=%async_computation.4 | async-start | bytes 4718592 | tf_op jit(solution)/shard_map/reduce_scatter | solution.py:61
  174.7 11.1 %collective-permute-start = (bf16[6,3,512]{0,2,1:T(8,128)(2,1)}, bf16[6,3,512]{0,2,1:T(8,128)(2,1)S(1)}, u32[]{:S(2)}, u32[]{:S(2)}) collective-permute-start(bf16[6,3,512]{0,2,1:T(8,128)(2,1)} %bitcast.1), channel_id=1, source_target_pairs={{0,8},{8,16},{16,24},{24,32},{32,40},{40,48},{48,56},{56,64},{64,7... | collective-permute-start | bytes 55304 | tf_op jit(solution)/shard_map/ppermute | solution.py:10
  194.6 4.9 %copy-start = (f32[512,3,512]{0,2,1:T(8,128)}, f32[512,3,512]{0,2,1:T(8,128)S(1)}, u32[]{:S(2)}) copy-start(f32[512,3,512]{0,2,1:T(8,128)S(1)} %fusion.16) | copy-start | bytes 9437188
  194.9 5.3 %collective-permute-start.1 = (bf16[127,512]{0,1:T(8,128)(2,1)S(1)}, bf16[127,512]{0,1:T(8,128)(2,1)S(1)}, u32[]{:S(2)}, u32[]{:S(2)}) collective-permute-start(bf16[127,512]{0,1:T(8,128)(2,1)S(1)} %slice_bitcast_fusion.128), channel_id=1, source_target_pairs={{0,8},{8,16},{16,24},{24,32},{32,40},{40,48},{48,56},{56,64},{64,7... | collective-permute-start | bytes 390152 | tf_op jit(solution)/shard_map/ppermute | solution.py:10
  243.3 3.3 copy-start.12
  246.6 9.6 %copy-start.9 = (bf16[16,512,1]{0,2,1:T(2,128)(2,1)S(1)}, bf16[16,512,1]{0,2,1:T(2,128)(2,1)}, u32[]{:S(2)}) copy-start(bf16[16,512,1]{0,2,1:T(2,128)(2,1)} %copy.22) | copy-start | bytes 49156
  249.7 15.3 %copy-start.8 = (bf16[16,512,1]{0,2,1:T(2,128)(2,1)S(1)}, bf16[16,512,1]{0,2,1:T(2,128)(2,1)}, u32[]{:S(2)}) copy-start(bf16[16,512,1]{0,2,1:T(2,128)(2,1)} %copy.19) | copy-start | bytes 49156
  252.9 3.2 copy-start.11
  265.0 9.5 %copy-start.7 = (bf16[16,512,1]{0,2,1:T(2,128)(2,1)S(1)}, bf16[16,512,1]{0,2,1:T(2,128)(2,1)}, u32[]{:S(2)}) copy-start(bf16[16,512,1]{0,2,1:T(2,128)(2,1)} %copy.16) | copy-start | bytes 49156
  274.5 9.7 %copy-start.6 = (bf16[16,512,1]{0,2,1:T(2,128)(2,1)S(1)}, bf16[16,512,1]{0,2,1:T(2,128)(2,1)}, u32[]{:S(2)}) copy-start(bf16[16,512,1]{0,2,1:T(2,128)(2,1)} %copy.34) | copy-start | bytes 49156
  284.2 9.5 %copy-start.5 = (bf16[16,512,1]{0,2,1:T(2,128)(2,1)S(1)}, bf16[16,512,1]{0,2,1:T(2,128)(2,1)}, u32[]{:S(2)}) copy-start(bf16[16,512,1]{0,2,1:T(2,128)(2,1)} %copy.31) | copy-start | bytes 49156
  293.7 9.5 %copy-start.4 = (bf16[16,512,1]{0,2,1:T(2,128)(2,1)S(1)}, bf16[16,512,1]{0,2,1:T(2,128)(2,1)}, u32[]{:S(2)}) copy-start(bf16[16,512,1]{0,2,1:T(2,128)(2,1)} %copy.28) | copy-start | bytes 49156
  303.3 9.7 %copy-start.3 = (bf16[16,512,1]{0,2,1:T(2,128)(2,1)S(1)}, bf16[16,512,1]{0,2,1:T(2,128)(2,1)}, u32[]{:S(2)}) copy-start(bf16[16,512,1]{0,2,1:T(2,128)(2,1)} %copy.25) | copy-start | bytes 49156
  313.0 9.5 %copy-start.2 = (bf16[16,512,1]{0,2,1:T(2,128)(2,1)S(1)}, bf16[16,512,1]{0,2,1:T(2,128)(2,1)}, u32[]{:S(2)}) copy-start(bf16[16,512,1]{0,2,1:T(2,128)(2,1)} %copy.37) | copy-start | bytes 49156
  322.5 9.8 %copy-start.10 = (f32[512]{0:T(512)S(1)}, f32[512]{0:T(512)}, u32[]{:S(2)}) copy-start(f32[512]{0:T(512)} %param.12) | copy-start | bytes 6148
  332.3 98.3 %copy-start.1 = (bf16[64,4096]{1,0:T(8,128)(2,1)S(1)}, bf16[64,4096]{1,0:T(8,128)(2,1)}, u32[]{:S(2)}) copy-start(bf16[64,4096]{1,0:T(8,128)(2,1)} %param.7) | copy-start | bytes 1572868
Sparse Core Ops, SparseCore 0:
  10.0 73.7 all-gather.3
  85.4 77.3 all-gather.5
  164.4 47.4 all-gather.7
  342.6 87.9 reduce-scatter.1
where the time goes:
time: 445 us; the launch traced here: 439 us
  waiting for transfers between devices  236 us (53%)
  matrix products  97.2 us (22%)
  local copies, waits for them, and re-layouts  70.7 us (16%)
  other arithmetic  14.6 us (3%)
  between operations  13.7 us (3%)
  starting transfers between devices  6.78 us (2%)
    reduce_scatter x1, waiting for transfers between devices, on_device(): lax.psum_scatter(jnp.dot(mixed_in, out_whole, preferred_element_type=jnp....  88.1 us
    all_gather x1, waiting for transfers between devices, on_device(): in_whole = lax.all_gather(in_weight, 'seq', axis=0, tiled=True)  79 us
    dot_general x8, matrix products, on_device(): jnp.einsum('jtc,jc->tc', stacked, long_filter[first_tap:first_tap + 16])  76.1 us
    all_gather x1, waiting for transfers between devices, on_device(): lax.all_gather(normed, 'tp', axis=0, tiled=True)  68 us
    unnamed x47, local copies, waits for them, and re-layouts  56.6 us
    dot_general x1, matrix products, on_device(): jnp.dot(lax.all_gather(normed, 'tp', axis=0, tiled=True), in_matrix, pref...  10.9 us
    dot_general x1, matrix products, on_device(): jnp.dot(mixed_in, out_whole, preferred_element_type=jnp.float32)  10.1 us
  transfers between devices with their start and end apart: 6, of which 4 were waited for; matrix products, arithmetic and copies ran while one was open for 37% of the time, Pallas kernels for 0%

commit v1 on v0

v1 whole, which is shorter than its diff:
```python
import functools

import jax
import jax.numpy as jnp
from jax import lax
from jax.experimental import pallas as pl
from jax.experimental.pallas import tpu as pltpu
from jax.sharding import PartitionSpec as P

MESH = pl.DeviceIdType.MESH
BF16 = jnp.bfloat16
F32 = jnp.float32

CHUNKS = 4
LANES = 128
HALO = 144
Z_FIRST = (1,)


def in_proj(normed, weights, branches, k):
    rows = normed.shape[0]

    def body(i, carry):
        at = pl.multiple_of(i * 256, 256)
        out = jnp.dot(normed[pl.ds(at, 256), :], weights[k], preferred_element_type=F32)
        branches[k, pl.ds(pl.multiple_of(HALO + at, 16), 256), :] = out.astype(BF16)
        return carry

    lax.fori_loop(0, rows // 256, body, 0)


def featurize(branches, short_ref, wide, query, gate, k):
    total = branches.shape[1]
    block = total - HALO

    def widen(i, carry):
        at = pl.multiple_of(i * 16, 16)
        for p in range(3):
            wide[p, pl.ds(at, 16), :] = branches[k, pl.ds(at, 16), p * LANES : (p + 1) * LANES].astype(F32)
        return carry

    lax.fori_loop(0, total // 16, widen, 0)
    taps = [[short_ref[j, p, k * LANES : (k + 1) * LANES][None] for j in range(7)] for p in range(3)]

    def filt(p, first, rows):
        out = taps[p][0] * wide[p, pl.ds(first, rows), :]
        for j in range(1, 7):
            out = out + taps[p][j] * wide[p, pl.ds(first - j, rows), :]
        return out

    def gates(i, carry):
        at = pl.multiple_of(i * 32, 32)
        value = filt(1, 16 + at, 32) * filt(2, 16 + at, 32)
        gate[pl.ds(at, 32), :] = value.astype(BF16).astype(F32)
        return carry

    lax.fori_loop(0, (block + 128) // 32, gates, 0)

    def queries(i, carry):
        at = pl.multiple_of(i * 32, 32)
        query[pl.ds(at, 32), :] = filt(0, HALO + at, 32)
        return carry

    lax.fori_loop(0, block // 32, queries, 0)


def long_conv(gate, query, long_ref, skip_ref, mixed, k):
    columns = slice(k * LANES, (k + 1) * LANES)
    block = query.shape[0]
    tile = 64

    def body(i, carry):
        at = pl.multiple_of(i * tile, tile)
        total = (long_ref[0:1, columns] + skip_ref[:, columns]) * gate[pl.ds(128 + at, tile), :]
        for j in range(1, 128):
            total = total + long_ref[j : j + 1, columns] * gate[pl.ds(128 + at - j, tile), :]
        mixed[pl.ds(at, tile), columns] = (query[pl.ds(at, tile), :] * total).astype(BF16)
        return carry

    lax.fori_loop(0, block // tile, body, 0)


def kernel(
    tokens,
    gain,
    in_w,
    short_ref,
    long_ref,
    skip_ref,
    out_w,
    result,
    normed,
    weights,
    out_weights,
    branches,
    wide,
    query,
    gate,
    mixed,
    part,
    landed,
    send_sems,
    w_sems,
    t_sems,
    h_sems,
    r_sems,
    l_sems,
):
    s, t = lax.axis_index("seq"), lax.axis_index("tp")
    z, xl, core = s // 4, (s // 2) % 2, s % 2
    xh, y = t // 4, t % 4

    def on_seq(dz, dx, dc):
        return ((z + dz) % 4) * 4 + ((xl + dx) % 2) * 2 + (core + dc) % 2

    def on_tp(dx, dy):
        return ((xh + dx) % 2) * 4 + (y + dy) % 4

    def seq_device(dz, dx, dc):
        return (on_seq(dz, dx, dc), t)

    def tp_device(dx, dy):
        return (s, on_tp(dx, dy))

    after = (lax.rem(s + 1, 16), t)
    before = (lax.rem(s + 15, 16), t)
    sibling = seq_device(0, 0, 1)

    partners = [sibling, seq_device(0, 1, 0), seq_device(1, 0, 0), seq_device(3, 0, 0), after, before]
    partners += [tp_device(dx, dy) for dx in range(2) for dy in range(4) if dx or dy]
    barrier = pltpu.get_barrier_semaphore()
    for partner in partners:
        pl.semaphore_signal(barrier, inc=1, device_id=partner, device_id_type=MESH)

    started = []

    def send(src, dst, recv_sem, device):
        copy = pltpu.make_async_remote_copy(
            src_ref=src,
            dst_ref=dst,
            send_sem=send_sems.at[len(started)],
            recv_sem=recv_sem,
            device_id=device,
            device_id_type=MESH,
        )
        copy.start()
        started.append(copy)

    def arrived(dst, recv_sem):
        pltpu.make_async_remote_copy(
            src_ref=dst,
            dst_ref=dst,
            send_sem=send_sems.at[0],
            recv_sem=recv_sem,
            device_id=sibling,
            device_id_type=MESH,
        ).wait_recv()

    local = []
    for k in range(CHUNKS):
        local.append(pltpu.make_async_copy(in_w.at[k], weights.at[k, pl.ds(pl.multiple_of(s * 256, 256), 256)], l_sems.at[k]))
    local.append(pltpu.make_async_copy(out_w, out_weights.at[s], l_sems.at[CHUNKS]))
    for copy in local:
        copy.start()

    own_rows = pl.multiple_of(t * 64, 64)
    for i in range(4):
        rows = tokens[i * 16 : (i + 1) * 16, :].astype(F32)
        scale = lax.rsqrt(jnp.mean(rows * rows, axis=-1, keepdims=True) + 1e-06)
        normed[pl.ds(own_rows + i * 16, 16), :] = (rows * scale * gain[...]).astype(BF16)

    pl.semaphore_wait(barrier, len(partners))

    def token_rows(dx, dy, half=None):
        first = on_tp(dx, dy) * 64
        if half is None:
            return normed.at[pl.ds(pl.multiple_of(first, 64), 64)]
        return normed.at[pl.ds(pl.multiple_of(first + 32 * half, 32), 32)]

    def t_round(dx):
        rows = token_rows(dx, 0)
        send(rows, rows, t_sems.at[dx, 3, 0], tp_device(0, 1))
        send(rows, rows, t_sems.at[dx, 1, 0], tp_device(0, 3))

    def t_pass(dx):
        arrived(token_rows(dx, 3), t_sems.at[dx, 3, 0])
        send(token_rows(dx, 3, 0), token_rows(dx, 3, 0), t_sems.at[dx, 2, 0], tp_device(0, 1))
        arrived(token_rows(dx, 1), t_sems.at[dx, 1, 0])
        send(token_rows(dx, 1, 1), token_rows(dx, 1, 1), t_sems.at[dx, 2, 1], tp_device(0, 3))

    def t_last(dx):
        for half in range(2):
            arrived(token_rows(dx, 2, half), t_sems.at[dx, 2, half])

    def shard(k, dz, dx, dc=0, half=None):
        origin = on_seq(dz, dx, dc)
        if k < CHUNKS:
            ref, depth = weights.at[k], 256
            first = origin * 256
        else:
            ref, depth = out_weights.at[origin], 512
            first = 0
        if half is None:
            return ref.at[pl.ds(pl.multiple_of(first, 256), depth)]
        return ref.at[pl.ds(pl.multiple_of(first + half * (depth // 2), 128), depth // 2)]

    def w_send(k, dz, dx, device, slot_dz, slot_dx, index=0, half=None):
        ref = shard(k, dz, dx, 0, half)
        send(ref, ref, w_sems.at[k, slot_dz, slot_dx, index], device)

    def w_arrived(k, dz, dx):
        if dz == 2 and (dx == 0 or k not in Z_FIRST):
            for half in range(2):
                arrived(shard(k, dz, dx, 0, half), w_sems.at[k, dz, dx, half])
        else:
            arrived(shard(k, dz, dx), w_sems.at[k, dz, dx, 0])

    def w_sibling(k, dz, dx):
        w_send(k, dz, dx, sibling, dz, dx, 2)

    def w_along_x(k, dz):
        w_send(k, dz, 0, seq_device(0, 1, 0), dz, 1)

    def w_round(k, dx):
        w_send(k, 0, dx, seq_device(1, 0, 0), 3, dx)
        w_send(k, 0, dx, seq_device(3, 0, 0), 1, dx)

    def w_pass(k, dz, dx):
        half = 0 if dz == 3 else 1
        w_send(k, dz, dx, seq_device(4 - dz, 0, 0), 2, dx, half, half)

    def w_start(k):
        local[k].wait()
        w_along_x(k, 0)
        w_round(k, 0)
        w_sibling(k, 0, 0)

    def w_second(k):
        if k in Z_FIRST:
            for dz in (3, 1):
                w_arrived(k, dz, 0)
                w_pass(k, dz, 0)
                w_along_x(k, dz)
                w_sibling(k, dz, 0)
        else:
            w_arrived(k, 0, 1)
            w_round(k, 1)
            w_sibling(k, 0, 1)
            for dz in (3, 1):
                w_arrived(k, dz, 0)
                w_pass(k, dz, 0)
                w_sibling(k, dz, 0)

    def w_third(k):
        if k in Z_FIRST:
            w_arrived(k, 2, 0)
            w_along_x(k, 2)
            w_sibling(k, 2, 0)
        else:
            for dz in (3, 1):
                w_arrived(k, dz, 1)
                w_pass(k, dz, 1)
                w_sibling(k, dz, 1)

    def w_fourth(k):
        if k in Z_FIRST:
            for dz in (0, 3, 1, 2):
                w_arrived(k, dz, 1)
                w_sibling(k, dz, 1)
        else:
            for dx in range(2):
                w_arrived(k, 2, dx)
                w_sibling(k, 2, dx)

    def w_from_sibling(k, dz, dx):
        arrived(shard(k, dz, dx, 1), w_sems.at[k, dz, dx, 2])

    def w_ready(k):
        for dz in range(4):
            for dx in range(2):
                w_from_sibling(k, dz, dx)

    def halo_send(k):
        block = branches.shape[1] - HALO
        send(branches.at[k, pl.ds(block, HALO)], branches.at[k, pl.ds(0, HALO)], h_sems.at[k], after)

    def halo_wait(k):
        arrived(branches.at[k, pl.ds(0, HALO)], h_sems.at[k])

        @pl.when(s == 0)
        def _():
            branches[k, 0:HALO, :] = jnp.zeros((HALO, branches.shape[2]), BF16)

    def project(k):
        in_proj(normed, weights, branches, k)
        halo_send(k)

    def mix(k):
        halo_wait(k)
        featurize(branches, short_ref, wide, query, gate, k)
        long_conv(gate, query, long_ref, skip_ref, mixed, k)

    send(token_rows(0, 0), token_rows(0, 0), t_sems.at[1, 0, 0], tp_device(1, 0))
    t_round(0)
    w_start(0)
    w_start(1)
    arrived(token_rows(1, 0), t_sems.at[1, 0, 0])
    t_round(1)
    w_second(0)
    w_start(2)
    t_pass(0)
    w_third(0)
    w_second(1)
    w_start(3)
    w_fourth(0)
    w_third(1)
    w_second(2)
    t_pass(1)
    t_last(0)
    w_start(4)
    w_fourth(1)
    t_last(1)
    w_ready(0)
    project(0)
    w_third(2)
    w_second(3)
    mix(0)
    w_fourth(2)
    w_third(3)
    w_ready(1)
    project(1)
    w_fourth(3)
    w_second(4)
    mix(1)
    w_third(4)
    w_ready(2)
    project(2)
    w_ready(3)
    project(3)
    mix(2)
    w_fourth(4)
    mix(3)

    groups = [(0, 0), (0, 1), (3, 0), (1, 0), (3, 1), (1, 1), (2, 0), (2, 1)]
    others = [(dx, dy) for dy in (2, 1, 3, 0) for dx in (1, 0) if dx or dy]

    def columns_of(dz, dx):
        return pl.ds(pl.multiple_of(on_seq(dz, dx, 0) // 2 * 512, 512), 512)

    for g, (dz, dx) in enumerate(groups):
        w_from_sibling(4, dz, dx)
        first = (on_seq(dz, dx, 0) // 2) * 2

        def out_proj(i, carry, first=first):
            origin = first + i
            out = jnp.dot(mixed[...], out_weights[origin], preferred_element_type=F32)
            part[:, pl.ds(pl.multiple_of(origin * 256, 256), 256)] = out.astype(BF16)
            return carry

        lax.fori_loop(0, 2, out_proj, 0)
        columns = columns_of(dz, dx)
        for n, (tx, ty) in enumerate(others):
            rows = pl.ds(pl.multiple_of(on_tp(tx, ty) * 64, 64), 64)
            send(part.at[rows, columns], landed.at[n, :, columns], r_sems.at[g, n], tp_device(tx, ty))

    for g, (dz, dx) in enumerate(groups):
        columns = columns_of(dz, dx)
        for n in range(len(others)):
            arrived(landed.at[n, :, columns], r_sems.at[g, n])
        total = tokens[:, columns].astype(F32) + part[pl.ds(own_rows, 64), columns].astype(F32)
        for n in range(len(others)):
            total = total + landed[n, :, columns].astype(F32)
        result[:, columns] = total.astype(BF16)

    for copy in started:
        copy.wait_send()


def on_device(tokens, norm_gain, in_weight, short_filter, long_filter, skip_gain, out_weight):
    depth, _, channels = in_weight.shape
    block = 512
    width = norm_gain.shape[0]
    chunked = in_weight.reshape(depth, 3, CHUNKS, LANES).transpose(2, 0, 1, 3).reshape(CHUNKS, depth, 3 * LANES)
    vmem = pl.BlockSpec(memory_space=pltpu.VMEM)
    hbm = pl.BlockSpec(memory_space=pl.ANY)
    return pl.pallas_call(
        kernel,
        out_shape=jax.ShapeDtypeStruct(tokens.shape, BF16),
        in_specs=[vmem, vmem, hbm, vmem, vmem, vmem, hbm],
        out_specs=vmem,
        scratch_shapes=[
            pltpu.VMEM((block, width), BF16),
            pltpu.VMEM((CHUNKS, width, 3 * LANES), BF16),
            pltpu.VMEM((16, channels, 256), BF16),
            pltpu.VMEM((CHUNKS, HALO + block, 3 * LANES), BF16),
            pltpu.VMEM((3, HALO + block, LANES), F32),
            pltpu.VMEM((block, LANES), F32),
            pltpu.VMEM((block + 128, LANES), F32),
            pltpu.VMEM((block, channels), BF16),
            pltpu.VMEM((block, width), BF16),
            pltpu.VMEM((7, 64, width), BF16),
            pltpu.SemaphoreType.DMA((180,)),
            pltpu.SemaphoreType.DMA((CHUNKS + 1, 4, 2, 3)),
            pltpu.SemaphoreType.DMA((2, 4, 2)),
            pltpu.SemaphoreType.DMA((CHUNKS,)),
            pltpu.SemaphoreType.DMA((8, 7)),
            pltpu.SemaphoreType.DMA((CHUNKS + 1,)),
        ],
        compiler_params=pltpu.CompilerParams(
            collective_id=0, has_side_effects=True, vmem_limit_bytes=58 * 2**20
        ),
        cost_estimate=pl.CostEstimate(flops=9_000_000_000, bytes_accessed=4_000_000, transcendentals=64),
    )(
        tokens,
        norm_gain.reshape(1, width),
        chunked,
        short_filter,
        long_filter,
        skip_gain.reshape(1, channels),
        out_weight,
    )


def solution(mesh):
    placed = (
        P(("seq", "tp"), None),
        P(),
        P("seq", None, "tp"),
        P(None, None, "tp"),
        P(None, "tp"),
        P("tp"),
        P("tp", "seq"),
    )
    return jax.shard_map(
        on_device, mesh=mesh, in_specs=placed, out_specs=P(("seq", "tp"), None), check_vma=False
    )
```

time: 445 us -> 154 us (0.35); the launches traced: 439 us -> 154 us
  waiting for transfers between devices: 236 us -> 0 us
  Pallas kernels: 0 us -> 149 us
  matrix products: 97.2 us -> 0 us
  local copies, waits for them, and re-layouts: 70.7 us -> 5.14 us
  other arithmetic: 14.6 us -> 0 us
  between operations: 13.7 us -> 0.03 us
  starting transfers between devices: 6.78 us -> 0 us
    pallas_call x0 -> x1, Pallas kernels: none -> 149 us  [on_device(): pl.pallas_call(kernel, out_shape=jax.ShapeDtypeStruct(tokens.shape, BF16)...]
    all_gather x3 -> x0, waiting for transfers between devices: 147 us -> none  [the longest x1 79 us: on_device(): in_whole = lax.all_gather(in_weight, 'seq', axis=0, tiled=True)]
    dot_general x10 -> x0, matrix products: 97.2 us -> none  [the longest x8 76.1 us: on_device(): jnp.einsum('jtc,jc->tc', stacked, long_filter[first_tap:first_tap + 16])]
    reduce_scatter x1 -> x0, waiting for transfers between devices: 88.1 us -> none  [on_device(): lax.psum_scatter(jnp.dot(mixed_in, out_whole, preferred_element_type=jnp....]
    unnamed x47 -> x5, local copies, waits for them, and re-layouts: 56.6 us -> 3.93 us
    slice x13 -> x0, local copies, waits for them, and re-layouts: 10.2 us -> none  [the longest x9 7.95 us: on_device(): long_filter[first_tap:first_tap + 16]]
    add x1 -> x0, other arithmetic: 7.91 us -> none  [featurize(): total + short_filter[delay] * widened[taps - 1 - delay:taps - 1 - delay +...]
    ppermute x2 -> x0, starting transfers between devices: 6.65 us -> none  [passed_along(): return lax.ppermute(x, axis, pairs)]
  transfers between devices with their start and end apart: 6 -> 0, of which waited for: 4 -> 0; matrix products, arithmetic and copies ran while one was open for 37% -> 0% of each run, Pallas kernels for 0% -> 0%
where the time goes in v1:
time: 154 us
  Pallas kernels  149 us (97%)
  local copies, waits for them, and re-layouts  5.14 us (3%)
    pallas_call x1, Pallas kernels, on_device(): pl.pallas_call(kernel, out_shape=jax.ShapeDtypeStruct(tokens.shape, BF16)...  149 us
    unnamed x5, local copies, waits for them, and re-layouts  3.93 us

profile of v1, /device:TPU:0, one launch (start us, length us, event | category | flops | bytes accessed | tf_op | source)
XLA Modules:
  0.0 154.1 jit_solution(18293437182963292139)
XLA Ops:
  0.0 1.4 copy.12
  1.4 0.1 copy.13
  1.5 0.0 copy-start
  1.5 1.2 copy.14.in_w
  2.6 0.0 copy-done
  2.6 0.7 copy.15.short_ref
  3.3 148.9 %shard_map.73 = bf16[64,4096]{1,0:T(8,128)(2,1)} custom-call(bf16[64,4096]{1,0:T(8,128)(2,1)} %tokens.1, f32[1,4096]{1,0:T(1,128)} %bitcast.8, bf16[4,256,384]{2,1,0:T(8,128)(2,1)} %copy.14.in_w, f32[7,3,512]{2,1,0:T(4,128)} %copy.15.short_ref, f32[128,512]{1,0:T(8,128)} %long_ref.1, f32[1,512]{1,0:T(1,128)} %bitcast.9, bf16[512,256]{1,0:T(8,128)(2,1)} %out_w.1), custom_call_target="tpu_custom_call" | custom-call | flops 8999999488 | bytes 4000000 | tf_op jit(solution)/shard_map/pallas_call | solution.py:386
  152.2 1.9 %copy.17 = bf16[64,4096]{1,0:T(8,128)(2,1)} copy(bf16[64,4096]{1,0:T(8,128)(2,1)} %shard_map.73) | data formatting | bytes 1048576
Async XLA Ops:
  1.5 1.2 copy-start

commit v2 on v1

v2 whole, which is shorter than its diff:
```python
import functools

import jax
import jax.numpy as jnp
from jax import lax
from jax.experimental import pallas as pl
from jax.experimental.pallas import tpu as pltpu
from jax.sharding import PartitionSpec as P

MESH = pl.DeviceIdType.MESH
BF16 = jnp.bfloat16
F32 = jnp.float32

CHUNKS = 4
LANES = 128
HALO = 144
Z_FIRST = (1,)
RS_X_FIRST = (1, 3, 5, 7)


def in_proj(normed, weights, wide, halo, k, half):
    rows = normed.shape[0] // 2
    slot = k % 2
    at = pl.multiple_of(half * rows, rows)
    out = jnp.dot(normed[pl.ds(at, rows), :], weights[k], preferred_element_type=F32).astype(BF16)
    for p in range(3):
        wide[slot, p, pl.ds(pl.multiple_of(HALO + at, 8), rows), :] = out[:, p * LANES : (p + 1) * LANES].astype(F32)

    @pl.when(half == 1)
    def _():
        halo[k, 0] = out[rows - HALO :]


def featurize(short_ref, halo, wide, query, gate, k, first_block):
    block = query.shape[1]
    slot = k % 2
    keep = jnp.where(first_block, 0.0, 1.0).astype(F32)
    for p in range(3):
        wide[slot, p, 0:HALO, :] = halo[k, 1, :, p * LANES : (p + 1) * LANES].astype(F32) * keep
    taps = [[short_ref[p, j : j + 1, k * LANES : (k + 1) * LANES] for j in range(7)] for p in range(3)]

    def filt(p, first, rows):
        out = taps[p][0] * wide[slot, p, pl.ds(first, rows), :]
        for j in range(1, 7):
            out = out + taps[p][j] * wide[slot, p, pl.ds(first - j, rows), :]
        return out

    def gates(i, carry):
        at = pl.multiple_of(i * 64, 64)
        value = filt(1, 16 + at, 64) * filt(2, 16 + at, 64)
        gate[k, pl.ds(at, 64), :] = value.astype(BF16).astype(F32)
        return carry

    lax.fori_loop(0, (block + 128) // 64, gates, 0)

    def queries(i, carry):
        at = pl.multiple_of(i * 64, 64)
        query[k, pl.ds(at, 64), :] = filt(0, HALO + at, 64)
        return carry

    lax.fori_loop(0, block // 64, queries, 0)


def long_conv(gate, query, long_ref, skip_ref, mixed, k, half):
    columns = slice(k * LANES, (k + 1) * LANES)
    rows = query.shape[1] // 2
    tile = 128

    def body(i, carry):
        at = pl.multiple_of(half * rows + i * tile, tile)

        def eight_taps(group, total):
            first = pl.multiple_of(group * 8, 8)
            taps = long_ref[pl.ds(first, 8), columns]
            for b in range(8):
                total = total + taps[b : b + 1] * gate[k, pl.ds(128 + at - first - b, tile), :]
            return total

        total = skip_ref[:, columns] * gate[k, pl.ds(128 + at, tile), :]
        total = lax.fori_loop(0, long_ref.shape[0] // 8, eight_taps, total)
        mixed[pl.ds(at, tile), columns] = (query[k, pl.ds(at, tile), :] * total).astype(BF16)
        return carry

    lax.fori_loop(0, rows // tile, body, 0)


def kernel(
    tokens,
    gain,
    in_w,
    short_ref,
    long_ref,
    skip_ref,
    out_w,
    result,
    normed,
    weights,
    out_weights,
    halo,
    wide,
    query,
    gate,
    mixed,
    part,
    over_x,
    over_y,
    send_sems,
    w_sems,
    t_sems,
    h_sems,
    r_sems,
    l_sems,
):
    s, t = lax.axis_index("seq"), lax.axis_index("tp")
    z, xl, core = s // 4, (s // 2) % 2, s % 2
    xh, y = t // 4, t % 4

    def on_seq(dz, dx, dc):
        return ((z + dz) % 4) * 4 + ((xl + dx) % 2) * 2 + (core + dc) % 2

    def on_tp(dx, dy):
        return ((xh + dx) % 2) * 4 + (y + dy) % 4

    def seq_device(dz, dx, dc):
        return (on_seq(dz, dx, dc), t)

    def tp_device(dx, dy):
        return (s, on_tp(dx, dy))

    after = (lax.rem(s + 1, 16), t)
    before = (lax.rem(s + 15, 16), t)
    sibling = seq_device(0, 0, 1)

    partners = [sibling, seq_device(0, 1, 0), seq_device(1, 0, 0), seq_device(3, 0, 0), after, before]
    partners += [tp_device(dx, dy) for dx in range(2) for dy in range(4) if dx or dy]
    barrier = pltpu.get_barrier_semaphore()
    for partner in partners:
        pl.semaphore_signal(barrier, inc=1, device_id=partner, device_id_type=MESH)

    started, loaded = [], []

    def send(src, dst, recv_sem, device):
        copy = pltpu.make_async_remote_copy(
            src_ref=src,
            dst_ref=dst,
            send_sem=send_sems.at[len(started)],
            recv_sem=recv_sem,
            device_id=device,
            device_id_type=MESH,
        )
        copy.start()
        started.append(copy)

    def arrived(dst, recv_sem):
        pltpu.make_async_remote_copy(
            src_ref=dst,
            dst_ref=dst,
            send_sem=send_sems.at[0],
            recv_sem=recv_sem,
            device_id=sibling,
            device_id_type=MESH,
        ).wait_recv()

    local = []
    for k in range(CHUNKS):
        rows = weights.at[k, pl.ds(pl.multiple_of(s * 256, 256), 256)]
        local.append(
            [
                pltpu.make_async_copy(
                    in_w.at[p, :, pl.ds(k * LANES, LANES)], rows.at[:, pl.ds(p * LANES, LANES)], l_sems.at[k, p]
                )
                for p in range(3)
            ]
        )
    local.append([pltpu.make_async_copy(out_w, out_weights.at[s], l_sems.at[CHUNKS, 0])])
    for copies in local:
        for copy in copies:
            copy.start()

    own_rows = pl.multiple_of(t * 64, 64)
    for i in range(4):
        rows = tokens[i * 16 : (i + 1) * 16, :].astype(F32)
        scale = lax.rsqrt(jnp.mean(rows * rows, axis=-1, keepdims=True) + 1e-06)
        normed[pl.ds(own_rows + i * 16, 16), :] = (rows * scale * gain[...]).astype(BF16)

    pl.semaphore_wait(barrier, len(partners))

    def token_rows(dx, dy, half=None):
        first = on_tp(dx, dy) * 64
        if half is None:
            return normed.at[pl.ds(pl.multiple_of(first, 64), 64)]
        return normed.at[pl.ds(pl.multiple_of(first + 32 * half, 32), 32)]

    def t_round(dx):
        rows = token_rows(dx, 0)
        send(rows, rows, t_sems.at[dx, 3, 0], tp_device(0, 1))
        send(rows, rows, t_sems.at[dx, 1, 0], tp_device(0, 3))

    def t_start():
        send(token_rows(0, 0), token_rows(0, 0), t_sems.at[1, 0, 0], tp_device(1, 0))
        t_round(0)

    def t_cross():
        arrived(token_rows(1, 0), t_sems.at[1, 0, 0])
        t_round(1)

    def t_pass(dx, dy):
        arrived(token_rows(dx, dy), t_sems.at[dx, dy, 0])
        half = 0 if dy == 3 else 1
        rows = token_rows(dx, dy, half)
        send(rows, rows, t_sems.at[dx, 2, half], tp_device(0, 4 - dy))

    def t_last(dx):
        for half in range(2):
            arrived(token_rows(dx, 2, half), t_sems.at[dx, 2, half])

    def shard(k, dz, dx, dc=0, half=None):
        origin = on_seq(dz, dx, dc)
        if k < CHUNKS:
            ref, depth = weights.at[k], 256
            first = origin * 256
        else:
            ref, depth = out_weights.at[origin], 512
            first = 0
        if half is None:
            return ref.at[pl.ds(pl.multiple_of(first, 256), depth)]
        return ref.at[pl.ds(pl.multiple_of(first + half * (depth // 2), 128), depth // 2)]

    def w_send(k, dz, dx, device, slot_dz, slot_dx, index=0, half=None):
        ref = shard(k, dz, dx, 0, half)
        send(ref, ref, w_sems.at[k, slot_dz, slot_dx, index], device)

    def w_arrived(k, dz, dx):
        if dz == 2 and (dx == 0 or k not in Z_FIRST):
            for half in range(2):
                arrived(shard(k, dz, dx, 0, half), w_sems.at[k, dz, dx, half])
        else:
            arrived(shard(k, dz, dx), w_sems.at[k, dz, dx, 0])

    def w_sibling(k, dz, dx):
        w_send(k, dz, dx, sibling, dz, dx, 2)

    def w_along_x(k, dz):
        w_send(k, dz, 0, seq_device(0, 1, 0), dz, 1)

    def w_round(k, dx):
        w_send(k, 0, dx, seq_device(1, 0, 0), 3, dx)
        w_send(k, 0, dx, seq_device(3, 0, 0), 1, dx)

    def w_pass(k, dz, dx):
        half = 0 if dz == 3 else 1
        w_send(k, dz, dx, seq_device(4 - dz, 0, 0), 2, dx, half, half)

    def w_own_x(k):
        if k not in loaded:
            loaded.append(k)
            for copy in local[k]:
                copy.wait()
        w_along_x(k, 0)

    def w_own_z(k):
        if k not in loaded:
            loaded.append(k)
            for copy in local[k]:
                copy.wait()
        w_round(k, 0)

    def w_x(k):
        w_arrived(k, 0, 1)
        w_round(k, 1)
        w_sibling(k, 0, 1)

    def w_z(k, dz):
        w_arrived(k, dz, 0)
        w_pass(k, dz, 0)
        if k in Z_FIRST:
            w_along_x(k, dz)
        w_sibling(k, dz, 0)

    def w_turn(k, dz):
        w_arrived(k, dz, 1)
        w_pass(k, dz, 1)
        w_sibling(k, dz, 1)

    def w_far(k, dx):
        w_arrived(k, 2, dx)
        if k in Z_FIRST:
            w_along_x(k, 2)
        w_sibling(k, 2, dx)

    def w_end(k, dz):
        w_arrived(k, dz, 1)
        w_sibling(k, dz, 1)

    def w_from_sibling(k, dz, dx):
        arrived(shard(k, dz, dx, 1), w_sems.at[k, dz, dx, 2])

    def w_ready(k):
        for dz in range(4):
            for dx in range(2):
                w_from_sibling(k, dz, dx)

    def half_of(side):
        return (xh + side) % 2

    def project(k, side):
        in_proj(normed, weights, wide, halo, k, half_of(side))

    def halo_send(k):
        send(halo.at[k, 0], halo.at[k, 1], h_sems.at[k], after)

    def feature(k):
        arrived(halo.at[k, 1], h_sems.at[k])
        featurize(short_ref, halo, wide, query, gate, k, s == 0)

    def conv(k, side):
        long_conv(gate, query, long_ref, skip_ref, mixed, k, half_of(side))

    groups = [(0, 0), (0, 1), (3, 0), (1, 0), (3, 1), (1, 1), (2, 0), (2, 1)]
    round_y = (2, 1, 3)

    def columns_of(g):
        return pl.ds(pl.multiple_of(on_seq(*groups[g], 0) // 2 * 512, 512), 512)

    def y_rows(dy):
        return pl.ds(pl.multiple_of((y + dy) % 4 * 64, 64), 64)

    def project_out(g, side):
        first = on_seq(*groups[g], 0) // 2 * 2
        half = half_of(side)

        def body(i, carry):
            origin = first + i
            rows = mixed[pl.ds(pl.multiple_of(half * 256, 256), 256), :]
            out = jnp.dot(rows, out_weights[origin], preferred_element_type=F32)
            part[half, :, pl.ds(pl.multiple_of(origin * 256, 256), 256)] = out.astype(BF16)
            return carry

        lax.fori_loop(0, 2, body, 0)

    def round_send(g, side, stage, slot):
        for dy in round_y:
            send(
                part.at[half_of(side), y_rows(dy), columns_of(g)],
                over_y.at[g, dy - 1, slot],
                r_sems.at[g, stage, dy - 1],
                tp_device(0, dy),
            )

    def round_arrived(g, stage, slot):
        for dy in round_y:
            arrived(over_y.at[g, dy - 1, slot], r_sems.at[g, stage, dy - 1])

    def emit(g, side):
        if side == 1:
            w_from_sibling(CHUNKS, *groups[g])
        project_out(g, side)
        if g not in RS_X_FIRST:
            round_send(g, side, 0 if side == 1 else 2, side)
        elif side == 1:
            send(part.at[half_of(1), :, columns_of(g)], over_x.at[g], r_sems.at[g, 0, 0], tp_device(1, 0))

    def stage_two(g):
        cols = columns_of(g)
        if g in RS_X_FIRST:
            arrived(over_x.at[g], r_sems.at[g, 0, 0])

            def body(i, carry):
                rows = pl.ds(pl.multiple_of(i * 64, 64), 64)
                both = part[xh, rows, cols].astype(F32) + over_x[g, rows, :].astype(F32)
                part[xh, rows, cols] = both.astype(BF16)
                return carry

            lax.fori_loop(0, 4, body, 0)
            round_send(g, 0, 1, 0)
        else:
            round_arrived(g, 0, 1)
            theirs = part[1 - xh, y_rows(0), cols].astype(F32)
            for dy in round_y:
                theirs = theirs + over_y[g, dy - 1, 1].astype(F32)
            part[1 - xh, y_rows(0), cols] = theirs.astype(BF16)
            send(part.at[1 - xh, y_rows(0), cols], over_x.at[g, pl.ds(0, 64)], r_sems.at[g, 1, 0], tp_device(1, 0))

    def finish(g):
        cols = columns_of(g)
        total = tokens[:, cols].astype(F32) + part[xh, y_rows(0), cols].astype(F32)
        round_arrived(g, 1 if g in RS_X_FIRST else 2, 0)
        for dy in round_y:
            total = total + over_y[g, dy - 1, 0].astype(F32)
        if g not in RS_X_FIRST:
            arrived(over_x.at[g, pl.ds(0, 64)], r_sems.at[g, 1, 0])
            total = total + over_x[g, 0:64, :].astype(F32)
        result[:, cols] = total.astype(BF16)

    t_start()
    w_own_x(0)
    w_own_z(0)
    w_sibling(0, 0, 0)
    w_own_x(1)
    w_own_z(1)
    w_sibling(1, 0, 0)
    w_own_z(2)
    w_sibling(2, 0, 0)
    w_own_z(3)
    w_sibling(3, 0, 0)
    w_own_x(2)
    w_z(0, 3)
    w_z(0, 1)
    w_own_x(3)
    w_z(1, 3)
    w_z(1, 1)
    t_pass(0, 3)
    t_pass(0, 1)
    t_cross()
    w_z(2, 3)
    w_z(2, 1)
    w_x(0)
    w_z(3, 3)
    w_z(3, 1)
    t_last(0)
    w_far(0, 0)
    w_end(1, 0)
    w_far(1, 0)
    w_far(2, 0)
    w_x(2)
    w_turn(0, 3)
    w_turn(0, 1)
    w_x(3)
    t_pass(1, 3)
    t_pass(1, 1)
    w_far(3, 0)
    w_end(1, 3)
    w_turn(2, 3)
    w_turn(2, 1)
    w_own_x(4)
    w_far(0, 1)
    w_end(1, 1)
    t_last(1)
    w_own_z(4)
    w_sibling(4, 0, 0)
    w_ready(0)
    project(0, 0)
    project(0, 1)
    w_end(1, 2)
    w_turn(3, 1)
    w_turn(3, 3)
    halo_send(0)
    w_far(2, 1)
    w_ready(1)
    project(1, 0)
    feature(0)
    w_ready(2)
    project(1, 1)
    halo_send(1)
    w_x(4)
    project(2, 0)
    w_z(4, 1)
    w_z(4, 3)
    feature(1)
    project(2, 1)
    w_far(3, 1)
    halo_send(2)
    conv(0, 1)
    w_ready(3)
    feature(2)
    project(3, 0)
    project(3, 1)
    halo_send(3)
    w_turn(4, 1)
    w_turn(4, 3)
    conv(1, 1)
    feature(3)
    w_far(4, 0)
    conv(2, 1)
    conv(3, 1)
    w_far(4, 1)
    emit(0, 1)
    emit(1, 1)
    emit(2, 1)
    emit(3, 1)
    emit(4, 1)
    emit(5, 1)
    emit(6, 1)
    stage_two(0)
    emit(7, 1)
    conv(0, 0)
    stage_two(2)
    conv(1, 0)
    stage_two(4)
    conv(2, 0)
    stage_two(6)
    conv(3, 0)
    emit(0, 0)
    emit(1, 0)
    stage_two(1)
    emit(2, 0)
    emit(3, 0)
    stage_two(3)
    emit(4, 0)
    emit(5, 0)
    emit(6, 0)
    emit(7, 0)
    finish(1)
    stage_two(5)
    finish(0)
    finish(3)
    stage_two(7)
    finish(2)
    finish(5)
    finish(4)
    finish(6)
    finish(7)
    for copy in started:
        copy.wait_send()


def on_device(tokens, norm_gain, in_weight, short_filter, long_filter, skip_gain, out_weight):
    channels = in_weight.shape[2]
    block = 512
    width = norm_gain.shape[0]
    vmem = pl.BlockSpec(memory_space=pltpu.VMEM)
    hbm = pl.BlockSpec(memory_space=pl.ANY)
    return pl.pallas_call(
        kernel,
        out_shape=jax.ShapeDtypeStruct(tokens.shape, BF16),
        in_specs=[vmem, vmem, hbm, vmem, vmem, vmem, hbm],
        out_specs=vmem,
        scratch_shapes=[
            pltpu.VMEM((block, width), BF16),
            pltpu.VMEM((CHUNKS, width, 3 * LANES), BF16),
            pltpu.VMEM((16, channels, 256), BF16),
            pltpu.VMEM((CHUNKS, 2, HALO, 3 * LANES), BF16),
            pltpu.VMEM((2, 3, HALO + block, LANES), F32),
            pltpu.VMEM((CHUNKS, block, LANES), F32),
            pltpu.VMEM((CHUNKS, block + 128, LANES), F32),
            pltpu.VMEM((block, channels), BF16),
            pltpu.VMEM((2, block // 2, width), BF16),
            pltpu.VMEM((8, block // 2, 512), BF16),
            pltpu.VMEM((8, 3, 2, 64, 512), BF16),
            pltpu.SemaphoreType.DMA((180,)),
            pltpu.SemaphoreType.DMA((CHUNKS + 1, 4, 2, 3)),
            pltpu.SemaphoreType.DMA((2, 4, 2)),
            pltpu.SemaphoreType.DMA((CHUNKS,)),
            pltpu.SemaphoreType.DMA((8, 3, 3)),
            pltpu.SemaphoreType.DMA((CHUNKS + 1, 3)),
        ],
        compiler_params=pltpu.CompilerParams(
            collective_id=0, has_side_effects=True, vmem_limit_bytes=58 * 2**20
        ),
        cost_estimate=pl.CostEstimate(flops=9_000_000_000, bytes_accessed=4_000_000, transcendentals=64),
    )(
        tokens,
        norm_gain.reshape(1, width),
        in_weight.transpose(1, 0, 2),
        short_filter.transpose(1, 0, 2),
        long_filter,
        skip_gain.reshape(1, channels),
        out_weight,
    )


def solution(mesh):
    placed = (
        P(("seq", "tp"), None),
        P(),
        P("seq", None, "tp"),
        P(None, None, "tp"),
        P(None, "tp"),
        P("tp"),
        P("tp", "seq"),
    )
    return jax.shard_map(
        on_device, mesh=mesh, in_specs=placed, out_specs=P(("seq", "tp"), None), check_vma=False
    )
```

time: 154 us -> 121 us (0.79)
  Pallas kernels: 149 us -> 119 us
  local copies, waits for them, and re-layouts: 5.14 us -> 1.87 us
    pallas_call x1, Pallas kernels: 149 us -> 119 us  [on_device(): pl.pallas_call(kernel, out_shape=jax.ShapeDtypeStruct(tokens.shape, BF16)...]
    unnamed x5 -> x1, local copies, waits for them, and re-layouts: 3.93 us -> 1.87 us
where the time goes in v2:
time: 121 us; the launch traced here: 120 us
  Pallas kernels  119 us (98%)
  local copies, waits for them, and re-layouts  1.87 us (2%)
    pallas_call x1, Pallas kernels, on_device(): pl.pallas_call(kernel, out_shape=jax.ShapeDtypeStruct(tokens.shape, BF16)...  119 us

profile of v2, /device:TPU:0, one launch (start us, length us, event | category | flops | bytes accessed | tf_op | source)
XLA Modules:
  0.0 120.4 jit_solution(1748518938303650364)
XLA Ops:
  0.0 118.5 %shard_map.73 = bf16[64,4096]{1,0:T(8,128)(2,1)} custom-call(bf16[64,4096]{1,0:T(8,128)(2,1)} %tokens.1, f32[1,4096]{1,0:T(1,128)} %bitcast.6, bf16[3,256,512]{2,1,0:T(8,128)(2,1)} %bitcast.4, f32[3,7,512]{2,1,0:T(8,128)} %bitcast.5, f32[128,512]{1,0:T(8,128)} %long_ref.1, f32[1,512]{1,0:T(1,128)} %bitcast.7, bf16[512,256]{1,0:T(8,128)(2,1)} %out_w.1), custom_call_target="tpu_custom_call" | custom-call | flops 8999999488 | bytes 4000000 | tf_op jit(solution)/shard_map/pallas_call | solution.py:523
  118.5 1.9 %copy.9 = bf16[64,4096]{1,0:T(8,128)(2,1)} copy(bf16[64,4096]{1,0:T(8,128)(2,1)} %shard_map.73) | data formatting | bytes 1048576

commit v3 on v2

--- a/solution.py
+++ b/solution.py
@@ -14,7 +14,7 @@
 CHUNKS = 4
 LANES = 128
 HALO = 144
-Z_FIRST = (1,)
+Z_FIRST = (2,)
 RS_X_FIRST = (1, 3, 5, 7)
 
 
@@ -393,22 +393,21 @@
         result[:, cols] = total.astype(BF16)
 
     t_start()
-    w_own_x(0)
     w_own_z(0)
     w_sibling(0, 0, 0)
-    w_own_x(1)
     w_own_z(1)
     w_sibling(1, 0, 0)
     w_own_z(2)
     w_sibling(2, 0, 0)
     w_own_z(3)
     w_sibling(3, 0, 0)
-    w_own_x(2)
+    w_own_x(0)
     w_z(0, 3)
     w_z(0, 1)
-    w_own_x(3)
+    w_own_x(1)
     w_z(1, 3)
     w_z(1, 1)
+    w_own_x(2)
     t_pass(0, 3)
     t_pass(0, 1)
     t_cross()
@@ -417,97 +416,98 @@
     w_x(0)
     w_z(3, 3)
     w_z(3, 1)
+    w_far(0, 0)
     t_last(0)
-    w_far(0, 0)
-    w_end(1, 0)
+    w_x(1)
     w_far(1, 0)
+    w_own_x(3)
+    w_own_x(4)
     w_far(2, 0)
-    w_x(2)
+    w_end(2, 0)
     w_turn(0, 3)
     w_turn(0, 1)
-    w_x(3)
+    w_end(2, 3)
+    w_far(3, 0)
     t_pass(1, 3)
     t_pass(1, 1)
-    w_far(3, 0)
-    w_end(1, 3)
-    w_turn(2, 3)
-    w_turn(2, 1)
-    w_own_x(4)
+    w_end(2, 1)
+    w_turn(1, 3)
+    w_turn(1, 1)
     w_far(0, 1)
-    w_end(1, 1)
-    t_last(1)
+    w_x(3)
     w_own_z(4)
     w_sibling(4, 0, 0)
+    w_far(1, 1)
     w_ready(0)
+    t_last(1)
     project(0, 0)
     project(0, 1)
-    w_end(1, 2)
+    halo_send(0)
+    w_ready(1)
+    project(1, 1)
+    w_turn(3, 3)
     w_turn(3, 1)
-    w_turn(3, 3)
-    halo_send(0)
-    w_far(2, 1)
-    w_ready(1)
     project(1, 0)
+    halo_send(1)
     feature(0)
+    w_x(4)
+    conv(0, 1)
+    feature(1)
+    conv(1, 1)
+    w_end(2, 2)
+    conv(0, 0)
+    w_z(4, 3)
+    w_z(4, 1)
+    conv(1, 0)
+    w_far(3, 1)
     w_ready(2)
-    project(1, 1)
-    halo_send(1)
-    w_x(4)
     project(2, 0)
-    w_z(4, 1)
-    w_z(4, 3)
-    feature(1)
     project(2, 1)
-    w_far(3, 1)
     halo_send(2)
-    conv(0, 1)
     w_ready(3)
-    feature(2)
     project(3, 0)
     project(3, 1)
     halo_send(3)
-    w_turn(4, 1)
-    w_turn(4, 3)
-    conv(1, 1)
+    feature(2)
+    conv(2, 1)
     feature(3)
-    w_far(4, 0)
-    conv(2, 1)
     conv(3, 1)
-    w_far(4, 1)
     emit(0, 1)
     emit(1, 1)
+    w_turn(4, 3)
+    w_turn(4, 1)
     emit(2, 1)
     emit(3, 1)
-    emit(4, 1)
-    emit(5, 1)
-    emit(6, 1)
-    stage_two(0)
-    emit(7, 1)
-    conv(0, 0)
-    stage_two(2)
-    conv(1, 0)
-    stage_two(4)
     conv(2, 0)
-    stage_two(6)
     conv(3, 0)
     emit(0, 0)
     emit(1, 0)
-    stage_two(1)
     emit(2, 0)
     emit(3, 0)
-    stage_two(3)
+    stage_two(0)
+    w_far(4, 0)
+    w_far(4, 1)
+    stage_two(1)
+    emit(4, 1)
+    emit(5, 1)
     emit(4, 0)
     emit(5, 0)
+    stage_two(2)
+    stage_two(3)
+    emit(6, 1)
+    emit(7, 1)
     emit(6, 0)
     emit(7, 0)
+    finish(0)
+    stage_two(4)
+    stage_two(5)
     finish(1)
-    stage_two(5)
-    finish(0)
+    finish(2)
     finish(3)
+    stage_two(6)
     stage_two(7)
-    finish(2)
+    finish(4)
     finish(5)
-    finish(4)
     finish(6)
     finish(7)
     for copy in started:

time: 121 us -> 118 us (0.975)
  Pallas kernels: 119 us -> 115 us
    pallas_call x1, Pallas kernels: 119 us -> 115 us  [on_device(): pl.pallas_call(kernel, out_shape=jax.ShapeDtypeStruct(tokens.shape, BF16)...]
where the time goes in v3:
time: 118 us; the launch traced here: 117 us
  Pallas kernels  115 us (97%)
  local copies, waits for them, and re-layouts  1.87 us (2%)
    pallas_call x1, Pallas kernels, on_device(): pl.pallas_call(kernel, out_shape=jax.ShapeDtypeStruct(tokens.shape, BF16)...  115 us

profile of v3, /device:TPU:0, one launch (start us, length us, event | category | flops | bytes accessed | tf_op | source)
XLA Modules:
  0.0 116.9 jit_solution(5532333982692344484)
XLA Ops:
  0.0 115.0 %shard_map.73 = bf16[64,4096]{1,0:T(8,128)(2,1)} custom-call(bf16[64,4096]{1,0:T(8,128)(2,1)} %tokens.1, f32[1,4096]{1,0:T(1,128)} %bitcast.6, bf16[3,256,512]{2,1,0:T(8,128)(2,1)} %bitcast.4, f32[3,7,512]{2,1,0:T(8,128)} %bitcast.5, f32[128,512]{1,0:T(8,128)} %long_ref.1, f32[1,512]{1,0:T(1,128)} %bitcast.7, bf16[512,256]{1,0:T(8,128)(2,1)} %out_w.1), custom_call_target="tpu_custom_call" | custom-call | flops 8999999488 | bytes 4000000 | tf_op jit(solution)/shard_map/pallas_call | solution.py:523
  115.0 1.9 %copy.9 = bf16[64,4096]{1,0:T(8,128)(2,1)} copy(bf16[64,4096]{1,0:T(8,128)(2,1)} %shard_map.73) | data formatting | bytes 1048576

commit v4 on v3

--- a/solution.py
+++ b/solution.py
@@ -480,32 +480,32 @@
     emit(3, 1)
     conv(2, 0)
     conv(3, 0)
+    w_far(4, 0)
+    w_far(4, 1)
     emit(0, 0)
     emit(1, 0)
+    stage_two(0)
+    stage_two(1)
     emit(2, 0)
     emit(3, 0)
-    stage_two(0)
-    w_far(4, 0)
-    w_far(4, 1)
-    stage_two(1)
     emit(4, 1)
     emit(5, 1)
     emit(4, 0)
     emit(5, 0)
-    stage_two(2)
-    stage_two(3)
     emit(6, 1)
     emit(7, 1)
     emit(6, 0)
     emit(7, 0)
+    stage_two(2)
+    stage_two(3)
     finish(0)
     stage_two(4)
     stage_two(5)
     finish(1)
+    stage_two(6)
+    stage_two(7)
     finish(2)
     finish(3)
-    stage_two(6)
-    stage_two(7)
     finish(4)
     finish(5)
     finish(6)

time: 118 us -> 117 us (level)
  no operation moved by 1% of the time
where the time goes in v4:
time: 117 us
  Pallas kernels  115 us (98%)
  local copies, waits for them, and re-layouts  1.87 us (2%)
    pallas_call x1, Pallas kernels, on_device(): pl.pallas_call(kernel, out_shape=jax.ShapeDtypeStruct(tokens.shape, BF16)...  115 us

profile of v4, /device:TPU:0, one launch (start us, length us, event | category | flops | bytes accessed | tf_op | source)
XLA Modules:
  0.0 116.9 jit_solution(12416730309168016942)
XLA Ops:
  0.0 115.0 %shard_map.73 = bf16[64,4096]{1,0:T(8,128)(2,1)} custom-call(bf16[64,4096]{1,0:T(8,128)(2,1)} %tokens.1, f32[1,4096]{1,0:T(1,128)} %bitcast.6, bf16[3,256,512]{2,1,0:T(8,128)(2,1)} %bitcast.4, f32[3,7,512]{2,1,0:T(8,128)} %bitcast.5, f32[128,512]{1,0:T(8,128)} %long_ref.1, f32[1,512]{1,0:T(1,128)} %bitcast.7, bf16[512,256]{1,0:T(8,128)(2,1)} %out_w.1), custom_call_target="tpu_custom_call" | custom-call | flops 8999999488 | bytes 4000000 | tf_op jit(solution)/shard_map/pallas_call | solution.py:523
  115.0 1.9 %copy.9 = bf16[64,4096]{1,0:T(8,128)(2,1)} copy(bf16[64,4096]{1,0:T(8,128)(2,1)} %shard_map.73) | data formatting | bytes 1048576

commit v5 on v4

--- a/solution.py
+++ b/solution.py
@@ -456,8 +456,6 @@
     conv(1, 1)
     w_end(2, 2)
     conv(0, 0)
-    w_z(4, 3)
-    w_z(4, 1)
     conv(1, 0)
     w_far(3, 1)
     w_ready(2)
@@ -468,6 +466,8 @@
     project(3, 0)
     project(3, 1)
     halo_send(3)
+    w_z(4, 3)
+    w_z(4, 1)
     feature(2)
     conv(2, 1)
     feature(3)

time: 117 us -> 117 us (level)
  no operation moved by 1% of the time
where the time goes in v5:
time: 117 us
  Pallas kernels  115 us (98%)
  local copies, waits for them, and re-layouts  1.87 us (2%)
    pallas_call x1, Pallas kernels, on_device(): pl.pallas_call(kernel, out_shape=jax.ShapeDtypeStruct(tokens.shape, BF16)...  115 us

profile of v5, /device:TPU:0, one launch (start us, length us, event | category | flops | bytes accessed | tf_op | source)
XLA Modules:
  0.0 116.8 jit_solution(16276425669063714129)
XLA Ops:
  0.0 115.0 %shard_map.73 = bf16[64,4096]{1,0:T(8,128)(2,1)} custom-call(bf16[64,4096]{1,0:T(8,128)(2,1)} %tokens.1, f32[1,4096]{1,0:T(1,128)} %bitcast.6, bf16[3,256,512]{2,1,0:T(8,128)(2,1)} %bitcast.4, f32[3,7,512]{2,1,0:T(8,128)} %bitcast.5, f32[128,512]{1,0:T(8,128)} %long_ref.1, f32[1,512]{1,0:T(1,128)} %bitcast.7, bf16[512,256]{1,0:T(8,128)(2,1)} %out_w.1), custom_call_target="tpu_custom_call" | custom-call | flops 8999999488 | bytes 4000000 | tf_op jit(solution)/shard_map/pallas_call | solution.py:523
  115.0 1.9 %copy.9 = bf16[64,4096]{1,0:T(8,128)(2,1)} copy(bf16[64,4096]{1,0:T(8,128)(2,1)} %shard_map.73) | data formatting | bytes 1048576
